TPU v7x, 32 devices: a whole 2x2x4 slice. The times are simulated.
32 devices in a mesh: groups: 2 (over y), row: 16 (over z, x, core).
Axes of the slice: x: 2, y: 2, z: 4, core: 2. Of those that a mesh axis runs over, the one named last changes fastest.
Arguments:
- left_features: bfloat16 [96, 4096], P(('groups', 'row')), parts along dimension 0, may hold values from -24 to 24
- right_features: bfloat16 [96, 4096], P(('groups', 'row')), parts along dimension 0, may hold values from -24 to 24
- alignment_mask: int32 [96, 128], P(('groups', 'row')), parts along dimension 0, may hold values from 0 to 1, as said below
- projection_weight: bfloat16 [1024, 128], replicated, may hold values from -0.1875 to 0.1875
- projection_bias: float32 [128], replicated, may hold values from -6 to 6
- pair_output_cotangent: bfloat16 [96, 48, 128], P(('groups', 'row')), parts along dimension 0, may hold values from -6 to 6
Outputs:
- pair_out: bfloat16 [96, 48, 128], P(('groups', 'row')), parts along dimension 0
- left_feature_gradient: float32 [96, 4096], P(('groups', 'row')), parts along dimension 0
- right_feature_gradient: float32 [96, 4096], P(('groups', 'row')), parts along dimension 0
- grad_weight: float32 [2048, 128], P('groups'), parts along dimension 0
- grad_bias: float32 [256], P('groups'), parts along dimension 0
There are 2 independent parts, one for each index of `groups`. A program takes and returns all parts, laid end to end along the dimension named above; an argument that names none is the same for every part. Nothing has to cross between parts.
Inputs may be any that keep to these rules, and one draw needn't show every extreme that they name: `alignment_mask`: each protein is present up to some length and padded after it: from some residue on to the last, all entries are 0; that length lies between 36 and 47.
All inputs are finite; a program needn't handle non-finite values.
Results may differ from a plain program's by a relative error of at most 0.0041.
Values may be sent and summed in bfloat16 or wider, within the bound.
A program may use at most 128 MiB of HBM per device.

v0:
```python
import math

import jax
import jax.numpy as jnp
from jax import lax
from jax.sharding import PartitionSpec as P


def local(
    left_features,
    right_features,
    alignment_mask,
    projection_weight,
    projection_bias,
    pair_output_cotangent,
):
    shard_rows, row_channel_width = left_features.shape
    alignment_depth = alignment_mask.shape[1]
    channel_count = row_channel_width // alignment_depth
    hidden_width = projection_weight.shape[0]
    pair_width = projection_weight.shape[1]
    mask_halfwidth = alignment_mask.astype(jnp.bfloat16)
    shard_mask = alignment_mask.astype(jnp.float32)
    left_masked = (
        left_features.reshape(shard_rows, alignment_depth, channel_count)
        * mask_halfwidth[:, :, None]
    )
    right_masked = (
        right_features.reshape(shard_rows, alignment_depth, channel_count)
        * mask_halfwidth[:, :, None]
    ).reshape(shard_rows, row_channel_width)
    gathered_right, gathered_mask = (
        lax.all_gather(right_masked, "row", axis=0, tiled=True),
        lax.all_gather(mask_halfwidth, "row", axis=0, tiled=True),
    )
    residues = gathered_right.shape[0]
    rows_per_block = math.gcd(residues, 128)
    number_of_blocks = residues // rows_per_block
    right_block_list = gathered_right.reshape(
        number_of_blocks, rows_per_block, alignment_depth, channel_count
    )
    mask_block_list = gathered_mask.reshape(number_of_blocks, rows_per_block, alignment_depth)
    cot_blocks = pair_output_cotangent.reshape(
        shard_rows, number_of_blocks, rows_per_block, pair_width
    ).transpose(1, 0, 2, 3)

    def block_step(state_carry, inputs):
        left_acc, weight_acc, bias_acc = state_carry
        right_blk, mask_blk, cot_blk = inputs
        counts = jnp.dot(
            shard_mask, mask_blk.astype(jnp.float32).T, precision=lax.Precision.HIGHEST
        )
        pair_norm = jnp.maximum(counts, 1.0)[:, :, None]
        outer_prod = jnp.einsum(
            "isc,jse->ijce", left_masked, right_blk, preferred_element_type=jnp.float32
        ).reshape(shard_rows, rows_per_block, hidden_width)
        prob = (outer_prod / pair_norm).astype(jnp.bfloat16)
        flat_prob = prob.reshape(shard_rows * rows_per_block, hidden_width)
        cot_flat = cot_blk.reshape(shard_rows * rows_per_block, pair_width)
        pair_block = (
            jnp.dot(flat_prob, projection_weight, preferred_element_type=jnp.float32)
            + projection_bias
        ).astype(jnp.bfloat16)
        prob_grad = lax.dot_general(
            cot_flat,
            projection_weight,
            (((1,), (1,)), ((), ())),
            preferred_element_type=jnp.float32,
        )
        outer_grad = (
            prob_grad.reshape(shard_rows, rows_per_block, hidden_width) / pair_norm
        ).astype(jnp.bfloat16)
        left_acc = left_acc + jnp.einsum(
            "ijce,jse->isc",
            outer_grad.reshape(shard_rows, rows_per_block, channel_count, channel_count),
            right_blk,
            preferred_element_type=jnp.float32,
        )
        weight_acc = weight_acc + lax.dot_general(
            flat_prob, cot_flat, (((0,), (0,)), ((), ())), preferred_element_type=jnp.float32
        )
        bias_acc = bias_acc + jnp.sum(cot_flat.astype(jnp.float32), axis=0)
        return (
            (left_acc, weight_acc, bias_acc),
            (pair_block.reshape(shard_rows, rows_per_block, pair_width), outer_grad),
        )

    starting_carry = (
        jnp.zeros((shard_rows, alignment_depth, channel_count), jnp.float32),
        jnp.zeros((hidden_width, pair_width), jnp.float32),
        jnp.zeros((pair_width,), jnp.float32),
    )
    (left_acc, weight_acc, bias_acc), (pairs, grads_out) = lax.scan(
        block_step, starting_carry, (right_block_list, mask_block_list, cot_blocks)
    )
    pair_out = pairs.transpose(1, 0, 2, 3).reshape(shard_rows, residues, pair_width)
    outer_all = grads_out.transpose(1, 0, 2, 3).reshape(
        shard_rows, residues, channel_count, channel_count
    )
    weight_sum, bias_sum = lax.psum((weight_acc, bias_acc), "row")
    left_feature_gradient = (left_acc * shard_mask[:, :, None]).reshape(
        shard_rows, row_channel_width
    )
    result = jnp.einsum("ijce,isc->jse", outer_all, left_masked, preferred_element_type=jnp.float32)
    right_accumulator = lax.psum_scatter(
        result.reshape(shard_rows * lax.axis_size("row"), row_channel_width),
        "row",
        scatter_dimension=0,
        tiled=True,
    ).reshape(shard_rows, alignment_depth, channel_count)
    right_feature_gradient = (right_accumulator * shard_mask[:, :, None]).reshape(
        shard_rows, row_channel_width
    )
    return (
        pair_out,
        left_feature_gradient,
        right_feature_gradient,
        weight_sum / residues,
        bias_sum / residues,
    )


def solution(mesh):
    in_specs = (
        P(("groups", "row"), None),
        P(("groups", "row"), None),
        P(("groups", "row"), None),
        P(),
        P(),
        P(("groups", "row"), None, None),
    )
    out_specs = (
        P(("groups", "row"), None, None),
        P(("groups", "row"), None),
        P(("groups", "row"), None),
        P("groups", None),
        P("groups"),
    )
    return jax.shard_map(local, mesh=mesh, in_specs=in_specs, out_specs=out_specs, check_vma=False)
```

profile of v0, /device:TPU:0, one launch (start us, length us, event | category | flops | bytes accessed | tf_op | source)
XLA Modules:
  0.0 182.3 jit_solution(10641527729326387571)
XLA Ops:
  7.3 0.8 fusion.19
  8.0 0.9 reshape.71
  9.4 0.8 multiply_bitcast_fusion
  10.2 24.6 %all-gather = bf16[16,3,4096]{2,1,0:T(4,128)(2,1)S(1)} all-gather(bf16[1,3,4096]{2,1,0:T(4,128)(2,1)S(1)} %multiply_bitcast_fusion), channel_id=1, replica_groups=mesh['groups'=2,'row'=16] {'row'}, dimensions={0}, use_global_device_ids=true | all-gather | bytes 417792 | tf_op jit(solution)/shard_map/all_gather | solution.py:33
  34.8 0.9 reshape.68
  35.7 0.7 copy.31
  36.4 17.5 %all-gather.1 = bf16[16,3,128]{2,1,0:T(4,128)(2,1)S(1)} all-gather(bf16[1,3,128]{2,1,0:T(4,128)(2,1)S(1)} %bitcast.117), channel_id=1, replica_groups=mesh['groups'=2,'row'=16] {'row'}, dimensions={0}, use_global_device_ids=true | all-gather | bytes 13056 | tf_op jit(solution)/shard_map/all_gather | solution.py:34
  53.9 17.4 %while.19 = (s32[]{:T(128)}, f32[3,128,32]{1,2,0:T(8,128)S(1)}, f32[1024,128]{1,0:T(8,128)S(1)}, f32[128]{0:T(128)S(1)}, bf16[3,3,16,128]{3,2,1,0:T(8,128)(2,1)S...) while((s32[]{:T(128)}, f32[3,128,32]{1,2,0:T(8,128)S(1)}, ...), condition=%wide.region_2.3_spmd.clone, body=%wide.region_0.2_spmd.clone.sunk | while | flops 63594672 | bytes 4620081 | solution.py:93
  54.0 0.7 convert_reduce_fusion.2
  54.7 1.2 bitcast_dynamic-update-slice_fusion.2
  56.1 0.3 fusion.45
  56.5 0.3 divide_convert_fusion.6
  56.8 0.3 copy.54
  57.1 0.4 reshape.95
  57.5 1.2 fusion.47
  58.9 0.4 convert_element_type.51
  59.3 0.3 convolution_add_fusion.3
  59.8 0.7 convert_reduce_fusion.2
  60.5 1.2 bitcast_dynamic-update-slice_fusion.2
  61.9 0.3 fusion.45
  62.3 0.3 divide_convert_fusion.6
  62.6 0.3 copy.54
  62.9 0.4 reshape.95
  63.3 1.2 fusion.47
  64.7 0.4 convert_element_type.51
  65.1 0.3 convolution_add_fusion.3
  65.6 0.7 convert_reduce_fusion.2
  66.3 1.2 bitcast_dynamic-update-slice_fusion.2
  67.8 0.3 fusion.45
  68.1 0.3 divide_convert_fusion.6
  68.4 0.3 copy.54
  68.7 0.4 reshape.95
  69.1 1.2 fusion.47
  70.5 0.4 convert_element_type.51
  70.9 0.3 convolution_add_fusion.3
  71.3 0.9 reshape.74
  72.2 1.5 copy.38
  73.7 1.5 convolution_bitcast_fusion.2
  75.2 2.0 %copy.39 = f32[48,128,32]{2,1,0:T(8,128)S(1)} copy(f32[48,128,32]{1,0,2:T(8,128)} %convolution_bitcast_fusion.2) | data formatting | bytes 1572864 | tf_op jit(solution)/shard_map/ijce,isc->jse/transpose | solution.py:104
  77.2 2.3 %reshape.75 = f32[48,4096]{1,0:T(8,128)} reshape(f32[48,128,32]{2,1,0:T(8,128)S(1)} %copy.39) | data formatting | bytes 1572864 | tf_op jit(solution)/shard_map/reshape | solution.py:106
  79.9 0.8 reshape.73
  80.7 0.6 copy.34
  81.3 0.6 dynamic-slice
  82.6 31.3 %psum.15 = f32[128]{0:T(128)S(1)} all-reduce(f32[128]{0:T(128)S(1)} %copy-done.2), channel_id=1, replica_groups=mesh['groups'=2,'row'=16] {'row'}, use_global_device_ids=true, to_apply=%region_5.6 | all-reduce | flops 128 | bytes 1024 | tf_op jit(solution)/shard_map/psum | solution.py:100
  113.9 0.5 broadcast_multiply_fusion.3
  114.4 57.6 %all-reduce.4.cloned.1.call-done = (f32[48,4096]{1,0:T(8,128)}, f32[1024,128]{1,0:T(8,128)}) async-done(((f32[48,4096]{1,0:T(8,128)}, f32[1024,128]{1,0:T(8,128)}), (f32[48,4096]{1,0:T(8,128)}, f32[1024,128]{1,0:T(8,128)})) %all-reduce.4.cloned.1.call-update) | async-done | bytes 1310736
  172.0 1.9 %broadcast_multiply_fusion = f32[1024,128]{1,0:T(8,128)} fusion(f32[1024,128]{1,0:T(8,128)} %get-tuple-element.176), kind=kLoop, calls=%fused_computation.32 | loop fusion | flops 131072 | bytes 1048576 | tf_op jit(solution)/shard_map/div | solution.py:118
  173.9 1.6 dynamic-slice_multiply_fusion
  (48 shorter events, 3.3 us)
Async XLA Ops:
  7.2 164.8 %all-reduce.4.cloned.1.call-start = ((), (), s32[]{:S(2)}) async-start(), calls=%async_computation | async-start | bytes 2621440
  34.8 19.1 %copy-start.3 = (f32[128]{0:T(128)S(1)}, f32[128]{0:T(128)}, u32[]{:S(2)}) copy-start(f32[128]{0:T(128)} %param.12) | copy-start | bytes 1540
  71.3 2.4 %copy-start = (f32[1024,128]{1,0:T(8,128)}, f32[1024,128]{1,0:T(8,128)S(1)}, u32[]{:S(2)}) copy-start(f32[1024,128]{1,0:T(8,128)S(1)} %get-tuple-element.79) | copy-start | bytes 1572868
  71.3 2.4 %copy-start.1 = (f32[128]{0:T(128)}, f32[128]{0:T(128)S(1)}, u32[]{:S(2)}) copy-start(f32[128]{0:T(128)S(1)} %get-tuple-element.80) | copy-start | bytes 1540
  79.5 1.8 %copy-start.4 = (u32[32]{0:T(128)S(1)}, u32[32]{0:T(128)}, u32[]{:S(2)}) copy-start(u32[32]{0:T(128)} %constant.39) | copy-start | bytes 388
  79.5 3.1 %copy-start.2 = (f32[128]{0:T(128)S(1)}, f32[128]{0:T(128)}, u32[]{:S(2)}) copy-start(f32[128]{0:T(128)} %copy-done.1) | copy-start | bytes 1540
Sparse Core Ops, SparseCore 0:
  79.6 92.3 all-reduce.3
where the time goes:
time: 183 us; the launch traced here: 182 us
  blocking collectives  73.3 us (40%)
  waiting for transfers between devices  57.7 us (32%)
  local copies, waits for them, and re-layouts  16.9 us (9%)
  between operations  14.9 us (8%)
  matrix products  11.4 us (6%)
  other arithmetic  7.93 us (4%)
    unnamed x2, waiting for transfers between devices  57.7 us
    psum x1, blocking collectives, local(): weight_sum, bias_sum = lax.psum((weight_acc, bias_acc), 'row')  31.3 us
    all_gather x1, blocking collectives, local(): lax.all_gather(right_masked, 'row', axis=0, tiled=True)  24.6 us
    all_gather x1, blocking collectives, local(): lax.all_gather(mask_halfwidth, 'row', axis=0, tiled=True)  17.5 us
  transfers between devices with their start and end apart: 1, of which 1 were waited for; matrix products, arithmetic and copies ran while one was open for 2% of the time, Pallas kernels for 0%

commit v1 on v0

--- a/solution.py
+++ b/solution.py
@@ -1,12 +1,338 @@
+import functools
 import math
 
 import jax
 import jax.numpy as jnp
 from jax import lax
+from jax.experimental import pallas as pl
+from jax.experimental.pallas import tpu as pltpu
 from jax.sharding import PartitionSpec as P
 
-
-def local(
+MESH = pl.DeviceIdType.MESH
+NT = (((1,), (1,)), ((), ()))
+TN = (((0,), (0,)), ((), ()))
+
+
+def gather_kernel(levels, pack_ref, out_ref, send_sem, recv_sem, own_sem):
+    group = lax.axis_index("groups")
+    me = lax.axis_index("row")
+    rows = pack_ref.shape[0]
+    half_rows = rows // 2
+    core = lax.rem(me, 2)
+    x = lax.rem(me // 2, 2)
+    z = me // 4
+
+    def rank(zz, xx, cc):
+        return zz * 4 + xx * 2 + cc
+
+    sib, xn = rank(z, x, 1 - core), rank(z, 1 - x, core)
+    up, dn = rank(z + 1, x, core), rank(z - 1, x, core)
+    has_up, has_dn = z < levels - 1, z > 0
+
+    barrier = pltpu.get_barrier_semaphore()
+
+    def greet(target):
+        pl.semaphore_signal(barrier, inc=1, device_id=(group, target), device_id_type=MESH)
+
+    greet(sib)
+    greet(xn)
+    pl.when(has_up)(lambda: greet(up))
+    pl.when(has_dn)(lambda: greet(dn))
+    own = pltpu.make_async_copy(pack_ref, out_ref.at[pl.ds(me * rows, rows)], own_sem)
+    own.start()
+    pl.semaphore_wait(barrier, 2 + has_up.astype(jnp.int32) + has_dn.astype(jnp.int32))
+
+    pending = []
+
+    def place(owner, half):
+        return out_ref.at[pl.ds(owner * rows + half * half_rows, half_rows)]
+
+    def copy_of(owner, half, target, index, local):
+        src = pack_ref.at[pl.ds(half * half_rows, half_rows)] if local else place(owner, half)
+        return pltpu.make_async_remote_copy(
+            src_ref=src,
+            dst_ref=place(owner, half),
+            send_sem=send_sem.at[index],
+            recv_sem=recv_sem.at[owner, half],
+            device_id=(group, target),
+            device_id_type=MESH,
+        )
+
+    def send(owner, half, target, cond=None, local=False):
+        copy = copy_of(owner, half, target, len(pending), local)
+        pending.append((copy, cond))
+        if cond is None:
+            copy.start()
+        else:
+            pl.when(cond)(copy.start)
+
+    def arrive(owner, half, cond=None):
+        copy = copy_of(owner, half, sib, 0, False)
+        if cond is None:
+            copy.wait_recv()
+        else:
+            pl.when(cond)(copy.wait_recv)
+
+    def both(a, b):
+        return a if b is None else jnp.logical_and(a, b)
+
+    send(me, 0, xn, local=True)
+    send(me, 1, up, has_up, local=True)
+    send(me, 1, dn, has_dn, local=True)
+    send(me, 0, up, has_up, local=True)
+    send(me, 0, dn, has_dn, local=True)
+    send(me, 1, xn, local=True)
+    send(me, 0, sib, local=True)
+    send(me, 1, sib, local=True)
+
+    arrive(xn, 0)
+    send(xn, 0, up, has_up)
+    send(xn, 0, dn, has_dn)
+    send(xn, 0, sib)
+
+    def from_level(k, sign, xx, half):
+        zo = z + sign * k
+        cond = zo >= 0 if sign < 0 else zo <= levels - 1
+        owner = rank(zo, xx, core)
+        arrive(owner, half, cond)
+        if half == 0 or xx is x:
+            onward, has_onward = (up, has_up) if sign < 0 else (dn, has_dn)
+            if k < levels - 1:
+                send(owner, half, onward, both(has_onward, cond))
+        if half == 1 and xx is x:
+            send(owner, half, xn, cond)
+        send(owner, half, sib, cond)
+
+    other = 1 - x
+    for k in range(1, levels):
+        for sign in (-1, 1):
+            from_level(k, sign, x, 1)
+        for sign in (-1, 1):
+            from_level(k, sign, x, 0)
+        if k == 1:
+            arrive(xn, 1)
+            send(xn, 1, sib)
+        for sign in (-1, 1):
+            from_level(k, sign, other, 0)
+        for sign in (-1, 1):
+            from_level(k, sign, other, 1)
+
+    for zz in range(levels):
+        for xx in range(2):
+            for half in range(2):
+                arrive(rank(zz, xx, 1 - core), half)
+    for copy, cond in pending:
+        if cond is None:
+            copy.wait_send()
+        else:
+            pl.when(cond)(copy.wait_send)
+    own.wait()
+
+
+def gather(pack, size):
+    levels = size // 4
+    rows, lanes = pack.shape
+    return pl.pallas_call(
+        functools.partial(gather_kernel, levels),
+        out_shape=jax.ShapeDtypeStruct((size * rows, lanes), pack.dtype),
+        in_specs=[pl.BlockSpec(memory_space=pltpu.VMEM)],
+        out_specs=pl.BlockSpec(memory_space=pltpu.VMEM),
+        scratch_shapes=[
+            pltpu.SemaphoreType.DMA((64,)),
+            pltpu.SemaphoreType.DMA((size, 2)),
+            pltpu.SemaphoreType.DMA,
+        ],
+        compiler_params=pltpu.CompilerParams(
+            collective_id=0, has_side_effects=True, vmem_limit_bytes=32 * 1024 * 1024
+        ),
+        name="gather",
+    )(pack)
+
+
+def compute_kernel(
+    n, sr, ch, rows, g, w_ref, bias_ref, pair_ref, lg_ref, rg_ref, gw_ref, gb_ref,
+    fa, fb, fc, mf, rn, bp, ap, wf, wl, wr, cb, t, acc,
+):
+    f32, bf16 = jnp.float32, jnp.bfloat16
+    me = lax.axis_index("row")
+    res = n * sr
+    pad = 64
+    lane = 128
+    hp = ch // 2
+    fr = sr * ch
+    cot_at, mask_at = 2 * fr, 2 * fr + sr * res
+
+    def dot(a, b, dims=(((1,), (0,)), ((), ()))):
+        return lax.dot_general(a, b, dims, preferred_element_type=f32)
+
+    mf[...] = jnp.zeros_like(mf)
+    for d in range(n):
+        base = d * rows
+        fa[d * fr:(d + 1) * fr] = g[base:base + fr].astype(f32)
+        fb[d * fr:(d + 1) * fr] = g[base + fr:base + 2 * fr].astype(f32)
+        fc[d * sr * res:(d + 1) * sr * res] = g[base + cot_at:base + mask_at].astype(f32)
+        m = g[base + mask_at:base + mask_at + 16].astype(f32)[:sr]
+        mf[d * sr:(d + 1) * sr] = m
+    masks = mf[...].astype(bf16)
+    rn[...] = 1.0 / jnp.maximum(dot(masks, jnp.concatenate([masks, masks], 0), NT), 1.0)
+
+    bp[...] = jnp.zeros_like(bp)
+    ap[...] = jnp.zeros_like(ap)
+    for e in range(ch):
+        bp[e * pad:e * pad + res] = fb[pl.ds(e, res, stride=ch), :].astype(bf16)
+        ap[e * pad:e * pad + res] = fa[pl.ds(e, res, stride=ch), :].astype(bf16)
+    wf[...] = w_ref[...].astype(f32)
+    for p in range(hp):
+        for h in range(2):
+            q = 2 * p + h
+            wl[p * ch:(p + 1) * ch, h * lane:(h + 1) * lane] = wf[pl.ds(q, ch, stride=ch), :].astype(bf16)
+            wr[p * ch:(p + 1) * ch, h * lane:(h + 1) * lane] = w_ref[q * ch:(q + 1) * ch]
+
+    gb_ref[...] = jnp.sum(fc[...], axis=0, keepdims=True) * (1.0 / res)
+    cb[...] = jnp.zeros_like(cb)
+    acc[...] = jnp.zeros_like(acc)
+
+    def fill_cot(k, block):
+        cb[k * lane:k * lane + res, 0:lane] = block
+        cb[k * lane + pad:k * lane + pad + res, lane:2 * lane] = block
+
+    def fill_prob(left, first, count):
+        for p in range(0, hp, 2):
+            o = dot(left, bp[p * lane:(p + 2) * lane], NT)
+            for k in range(count):
+                scale = rn[pl.ds(first + k, 1), :]
+                for u in range(2):
+                    t[(p + u) * ch:(p + u + 1) * ch, k * lane:(k + 1) * lane] = (
+                        o[k * ch:(k + 1) * ch, u * lane:(u + 1) * lane] * scale
+                    ).astype(bf16)
+
+    def step(v, carry):
+        base = pl.multiple_of(v * (2 * rows), 16)
+        left = jnp.concatenate([g[pl.ds(base, fr)], g[pl.ds(base + rows, fr)]], 0)
+        fill_prob(left, v * (2 * sr), 2 * sr)
+        for k in range(2 * sr):
+            fill_cot(k, g[pl.ds(base + (k // sr) * rows + cot_at + (k % sr) * res, res)])
+        acc[...] += dot(t[...], cb[...])
+        return carry
+
+    lax.fori_loop(0, n // 2, step, 0)
+    for p in range(hp):
+        for h in range(2):
+            gw_ref[pl.ds(2 * p + h, ch, stride=ch), :] = (
+                acc[p * ch:(p + 1) * ch, h * lane:(h + 1) * lane] * (1.0 / res)
+            )
+
+    base = pl.multiple_of(me * rows, 16)
+    width = sr * lane
+    scales = jnp.concatenate([rn[pl.ds(me * sr + k, 1), :] for k in range(sr)], 1)
+
+    def side(weights, features):
+        og = (dot(weights, cb[:width], NT) * scales).astype(bf16)
+        flat = jnp.concatenate(
+            [
+                jnp.concatenate(
+                    [og[p * ch:(p + 1) * ch, k * lane:(k + 1) * lane] for p in range(hp)], 1
+                )
+                for k in range(sr)
+            ],
+            0,
+        )
+        return dot(flat, features[...])
+
+    fill_prob(g[pl.ds(base, fr)], me * sr, sr)
+    for k in range(sr):
+        fill_cot(k, g[pl.ds(base + cot_at + k * res, res)])
+    pairs = dot(t[:, :width], wl[...], TN)
+    lg = side(wl[...], bp)
+    for k in range(sr):
+        pair_ref[k * res:(k + 1) * res] = (
+            pairs[k * lane:k * lane + res, :lane]
+            + pairs[k * lane + pad:k * lane + pad + res, lane:]
+            + bias_ref[...]
+        ).astype(bf16)
+        lg_ref[k * ch:(k + 1) * ch] = lg[k * ch:(k + 1) * ch] * mf[pl.ds(me * sr + k, 1), :]
+    for k in range(sr):
+        fill_cot(k, fc[pl.ds(me * sr + k, res, stride=res), :].astype(bf16))
+    rg = side(wr[...], ap)
+    for k in range(sr):
+        rg_ref[k * ch:(k + 1) * ch] = rg[k * ch:(k + 1) * ch] * mf[pl.ds(me * sr + k, 1), :]
+
+
+def compute(g, weight, bias, n, sr, ch, rows):
+    f32, bf16 = jnp.float32, jnp.bfloat16
+    res, hidden, lane = n * sr, ch * ch, 128
+    vmem = pl.BlockSpec(memory_space=pltpu.VMEM)
+    return pl.pallas_call(
+        functools.partial(compute_kernel, n, sr, ch, rows),
+        out_shape=(
+            jax.ShapeDtypeStruct((sr * res, lane), bf16),
+            jax.ShapeDtypeStruct((sr * ch, lane), f32),
+            jax.ShapeDtypeStruct((sr * ch, lane), f32),
+            jax.ShapeDtypeStruct((hidden, lane), f32),
+            jax.ShapeDtypeStruct((1, lane), f32),
+        ),
+        in_specs=[vmem] * 3,
+        out_specs=(vmem,) * 5,
+        scratch_shapes=[
+            pltpu.VMEM((res * ch, lane), f32),
+            pltpu.VMEM((res * ch, lane), f32),
+            pltpu.VMEM((res * res, lane), f32),
+            pltpu.VMEM((64, lane), f32),
+            pltpu.VMEM((64, lane), f32),
+            pltpu.VMEM((ch * 64, lane), bf16),
+            pltpu.VMEM((ch * 64, lane), bf16),
+            pltpu.VMEM((hidden, lane), f32),
+            pltpu.VMEM((hidden // 2, 2 * lane), bf16),
+            pltpu.VMEM((hidden // 2, 2 * lane), bf16),
+            pltpu.VMEM((2 * sr * lane, 2 * lane), bf16),
+            pltpu.VMEM((hidden // 2, 2 * sr * lane), bf16),
+            pltpu.VMEM((hidden // 2, 2 * lane), f32),
+        ],
+        compiler_params=pltpu.CompilerParams(vmem_limit_bytes=40 * 1024 * 1024),
+        name="compute",
+    )(g, weight, bias)
+
+
+def gathered_local(
+    left_features,
+    right_features,
+    alignment_mask,
+    projection_weight,
+    projection_bias,
+    pair_output_cotangent,
+):
+    sr, width = left_features.shape
+    depth = alignment_mask.shape[1]
+    ch = width // depth
+    n = lax.axis_size("row")
+    res = n * sr
+    mask = alignment_mask.astype(jnp.bfloat16)
+
+    def by_channel(features):
+        masked = features.reshape(sr, depth, ch) * mask[:, :, None]
+        return masked.transpose(0, 2, 1).reshape(sr * ch, depth)
+
+    parts = [
+        by_channel(left_features),
+        by_channel(right_features),
+        pair_output_cotangent.reshape(sr * res, -1),
+        mask,
+    ]
+    used = sum(part.shape[0] for part in parts)
+    rows = -(-used // 32) * 32
+    parts.append(jnp.zeros((rows - used, depth), jnp.bfloat16))
+    pack = jnp.concatenate(parts, 0)
+    pair, lg, rg, gw, gb = compute(
+        gather(pack, n), projection_weight, projection_bias.reshape(1, -1), n, sr, ch, rows
+    )
+
+    def by_row(grad):
+        return grad.reshape(sr, ch, depth).transpose(0, 2, 1).reshape(sr, width)
+
+    return pair.reshape(sr, res, -1), by_row(lg), by_row(rg), gw, gb.reshape(-1)
+
+
+def streamed_local(
     left_features,
     right_features,
     alignment_mask,
@@ -136,4 +462,16 @@
         P("groups", None),
         P("groups"),
     )
+    size = mesh.shape["row"]
+
+    def local(left, right, mask, weight, bias, cot):
+        sr, depth = mask.shape
+        ch = left.shape[1] // depth
+        res = sr * size
+        fits = (
+            size == 16 and res % 16 == 0 and res <= 64 and ch == 32 and (sr * ch) % 16 == 0
+            and depth == 128 and cot.shape[2] == 128 and sr <= 16
+        )
+        return (gathered_local if fits else streamed_local)(left, right, mask, weight, bias, cot)
+
     return jax.shard_map(local, mesh=mesh, in_specs=in_specs, out_specs=out_specs, check_vma=False)

time: 183 us -> 34.7 us (0.19)
  blocking collectives: 73.3 us -> 0 us
  waiting for transfers between devices: 57.7 us -> 0 us
  Pallas kernels: 0 us -> 28.1 us
  between operations: 14.9 us -> 0.73 us
  local copies, waits for them, and re-layouts: 16.9 us -> 4.68 us
  matrix products: 11.4 us -> 0 us
  other arithmetic: 7.93 us -> 0.85 us
    unnamed x2 -> x0, waiting for transfers between devices: 57.7 us -> none
    all_gather x2 -> x0, blocking collectives: 42 us -> none  [the longest x1 24.6 us: local(): lax.all_gather(right_masked, 'row', axis=0, tiled=True)]
    psum x1 -> x0, blocking collectives: 31.3 us -> none  [local(): weight_sum, bias_sum = lax.psum((weight_acc, bias_acc), 'row')]
    pallas_call x0 -> x2, Pallas kernels: none -> 28.1 us  [the longest x1 19.1 us: gather(): pl.pallas_call(functools.partial(gather_kernel, levels), out_shape=jax.Sh...]
    dot_general x19 -> x0, matrix products: 11.4 us -> none  [the longest x3 3.53 us: block_step(): jnp.dot(flat_prob, projection_weight, preferred_element_type=jnp.float32)]
    reshape x13 -> x6, local copies, waits for them, and re-layouts: 9.06 us -> 3.55 us  [the longest x4 1.8 us: by_row(): return grad.reshape(sr, ch, depth).transpose(0, 2, 1).reshape(sr, width)]
    transpose x6 -> x2, local copies, waits for them, and re-layouts: 3.42 us -> 0.18 us  [by_channel(): return masked.transpose(0, 2, 1).reshape(sr * ch, depth)]
    div x2 -> x0, other arithmetic: 2.4 us -> none  [the longest x1 1.88 us: local(): weight_sum / residues]
  transfers between devices with their start and end apart: 1 -> 0, of which waited for: 1 -> 0; matrix products, arithmetic and copies ran while one was open for 2% -> 0% of each run, Pallas kernels for 0% -> 0%
where the time goes in v1:
time: 34.7 us; the launch traced here: 34.4 us
  Pallas kernels  28.1 us (81%)
  local copies, waits for them, and re-layouts  4.68 us (13%)
  other arithmetic  0.85 us (2%)
  between operations  0.73 us (2%)
    pallas_call x1, Pallas kernels, gather(): pl.pallas_call(functools.partial(gather_kernel, levels), out_shape=jax.Sh...  19.1 us
    pallas_call x1, Pallas kernels, compute(): pl.pallas_call(functools.partial(compute_kernel, n, sr, ch, rows), out_sh...  9.06 us
    reshape x4, local copies, waits for them, and re-layouts, by_row(): return grad.reshape(sr, ch, depth).transpose(0, 2, 1).reshape(sr, width)  1.8 us
    reshape x2, local copies, waits for them, and re-layouts, by_channel(): masked = features.reshape(sr, depth, ch) * mask[:, :, None]  1.75 us
    concatenate x1, local copies, waits for them, and re-layouts, gathered_local(): pack = jnp.concatenate(parts, 0)  0.94 us
    convert_element_type x1, other arithmetic, gathered_local(): mask = alignment_mask.astype(jnp.bfloat16)  0.73 us

profile of v1, /device:TPU:0, one launch (start us, length us, event | category | flops | bytes accessed | tf_op | source)
XLA Modules:
  0.0 34.4 jit_solution(987054337729529721)
XLA Ops:
  0.6 0.0 copy-start.1
  0.6 0.0 copy-start
  0.7 0.7 %convert_element_type.3 = bf16[3,128]{1,0:T(4,128)(2,1)S(1)} convert(s32[3,128]{1,0:T(4,128)} %param.8) | non-fusion elementwise | flops 384 | bytes 2304 | tf_op jit(solution)/shard_map/convert_element_type | solution.py:309
  1.4 0.9 %reshape.47 = bf16[3,128,32]{2,1,0:T(8,128)(2,1)S(1)} reshape(bf16[3,4096]{1,0:T(4,128)(2,1)} %param.6) | data formatting | bytes 49152 | tf_op jit(solution)/shard_map/reshape | solution.py:312
  2.3 0.9 %reshape.49 = bf16[3,128,32]{2,1,0:T(8,128)(2,1)S(1)} reshape(bf16[3,4096]{1,0:T(4,128)(2,1)} %param.7) | data formatting | bytes 49152 | tf_op jit(solution)/shard_map/reshape | solution.py:312
  3.1 0.1 multiply_bitcast_fusion
  3.3 0.1 copy.16
  3.4 0.1 copy.15
  3.5 0.9 %concatenate.3.pack_ref = bf16[352,128]{1,0:T(8,128)(2,1)S(1)} concatenate(bf16[96,128]{1,0:T(8,128)(2,1)S(1)} %bitcast.20, bf16[96,128]{1,0:T(8,128)(2,1)S(1)} %bitcast.19, bf16[144,128]{1,0:T(8,128)(2,1)} %bitcast.21, bf16[3,128]{1,0:T(4,128)(2,1)S(1)} %convert_element_type.3, bf16[13,128]{1,0:T(8,128)(2,1)S(1)} %broadcast_in_dim.2), dimensions={0} | concatenate | bytes 180224 | tf_op jit(solution)/shard_map/concatenate | solution.py:324
  4.4 19.1 %gather.1.g = bf16[5632,128]{1,0:T(8,128)(2,1)S(1)} custom-call(bf16[352,128]{1,0:T(8,128)(2,1)S(1)} %concatenate.3.pack_ref), custom_call_target="tpu_custom_call" | custom-call | tf_op jit(solution)/shard_map/gather/pallas_call | solution.py:135
  23.5 0.0 copy-done.1
  23.5 0.0 copy-done
  23.5 9.1 %compute.1 = (bf16[144,128]{1,0:T(8,128)(2,1)}, f32[96,128]{1,0:T(8,128)S(1)}, f32[96,128]{1,0:T(8,128)S(1)}, f32[1024,128]{1,0:T(8,128)}, f32[1,128]{1,0:T(1,128)}) custom-call(bf16[5632,128]{1,0:T(8,128)(2,1)S(1)} %gather.1.g, bf16[1024,128]{1,0:T(8,128)(2,1)S(1)} %copy-done, f32[1,128]{1,0:T(1,128)S(1)} %bitcast.16), custom_call_target="tpu_custom_call" | custom-call | tf_op jit(solution)/shard_map/compute/pallas_call | solution.py:265
  32.6 0.1 copy.17
  32.7 0.8 %reshape.55 = f32[3,4096]{1,0:T(4,128)} reshape(f32[3,128,32]{2,1,0:T(8,128)S(1)} %bitcast.17) | data formatting | bytes 98304 | tf_op jit(solution)/shard_map/reshape | solution.py:330
  33.5 0.1 copy.18
  33.6 0.8 %reshape.57 = f32[3,4096]{1,0:T(4,128)} reshape(f32[3,128,32]{2,1,0:T(8,128)S(1)} %bitcast.18) | data formatting | bytes 98304 | tf_op jit(solution)/shard_map/reshape | solution.py:330
  (1 shorter events, 0.0 us)
Async XLA Ops:
  0.6 22.9 %copy-start.1 = (f32[128]{0:T(128)S(1)}, f32[128]{0:T(128)}, u32[]{:S(2)}) copy-start(f32[128]{0:T(128)} %param.10) | copy-start | bytes 1540
  0.6 22.9 %copy-start = (bf16[1024,128]{1,0:T(8,128)(2,1)S(1)}, bf16[1024,128]{1,0:T(8,128)(2,1)}, u32[]{:S(2)}) copy-start(bf16[1024,128]{1,0:T(8,128)(2,1)} %w_ref.1) | copy-start | bytes 786436

commit v2 on v0

--- a/solution.py
+++ b/solution.py
@@ -1,12 +1,375 @@
+import functools
 import math
 
 import jax
 import jax.numpy as jnp
 from jax import lax
+from jax.experimental import pallas as pl
+from jax.experimental.pallas import tpu as pltpu
 from jax.sharding import PartitionSpec as P
 
-
-def local(
+MESH = pl.DeviceIdType.MESH
+NT = (((1,), (1,)), ((), ()))
+TN = (((0,), (0,)), ((), ()))
+
+
+def dot(a, b, dims=(((1,), (0,)), ((), ()))):
+    return lax.dot_general(a, b, dims, preferred_element_type=jnp.float32)
+
+
+def fused_kernel(
+    levels, n, sr, ch,
+    left_ref, right_ref, mask_ref, w_ref, bias_ref, cot_ref,
+    pair_ref, lg_ref, rg_ref, gw_ref, gb_ref,
+    gf, gc, fa, fb, fc, mf, rn, bp, ap, wf, wl, wr, cb, t, acc, xf, m16,
+    send_sem, recv_sem,
+):
+    f32, bf16 = jnp.float32, jnp.bfloat16
+    group = lax.axis_index("groups")
+    me = lax.axis_index("row")
+    res, pad, lane, hp = n * sr, 64, 128, ch // 2
+    fr = sr * ch
+    rows = 2 * fr + 16
+    q = lane // ch
+    core, x, z = lax.rem(me, 2), lax.rem(me // 2, 2), me // 4
+    other = 1 - x
+
+    def rank(zz, xx, cc):
+        return zz * 4 + xx * 2 + cc
+
+    sib, xn = rank(z, x, 1 - core), rank(z, other, core)
+    up, dn = rank(z + 1, x, core), rank(z - 1, x, core)
+    has_up, has_dn = z < levels - 1, z > 0
+
+    barrier = pltpu.get_barrier_semaphore()
+
+    def greet(target):
+        pl.semaphore_signal(barrier, inc=1, device_id=(group, target), device_id_type=MESH)
+
+    greet(sib)
+    greet(xn)
+    pl.when(has_up)(lambda: greet(up))
+    pl.when(has_dn)(lambda: greet(dn))
+
+    m16[...] = jnp.zeros_like(m16)
+    m16[:sr] = mask_ref[...].astype(f32)
+    row_at = lax.broadcasted_iota(jnp.int32, (lane, lane), 0)
+    lane_at = lax.broadcasted_iota(jnp.int32, (lane, lane), 1)
+    order = ((row_at % q) * (lane // q) + row_at // q == lane_at).astype(bf16)
+    own_mask = dot(m16[...].astype(bf16), order)
+    slot = pl.multiple_of(me * rows, 16)
+    gf[pl.ds(slot + 2 * fr, 16)] = own_mask.astype(bf16)
+    xf[...] = jnp.zeros_like(xf)
+    for side_index, ref in enumerate((left_ref, right_ref)):
+        for h in range(ch):
+            xf[pl.ds(h, sr, stride=ch), :] = ref[:, h * lane:(h + 1) * lane].astype(f32)
+        turned = xf[...].T
+        for i in range(sr):
+            block = jnp.concatenate(
+                [turned[u * ch:(u + 1) * ch, i * ch:(i + 1) * ch] for u in range(q)], 1
+            )
+            gf[pl.ds(slot + side_index * fr + i * ch, ch)] = (block * own_mask[i:i + 1]).astype(bf16)
+    gc[pl.ds(pl.multiple_of(me * sr * res, 16), sr * res)] = cot_ref[...]
+
+    pl.semaphore_wait(barrier, 2 + has_up.astype(jnp.int32) + has_dn.astype(jnp.int32))
+
+    pending = []
+    split = res
+    FEATURES, COT_X, COT_Z = 0, 1, 2
+
+    def place(owner, piece):
+        if piece == FEATURES:
+            return gf.at[pl.ds(pl.multiple_of(owner * rows, 16), rows)]
+        first = pl.multiple_of(owner * sr * res, 16)
+        if piece == COT_X:
+            return gc.at[pl.ds(first, split)]
+        return gc.at[pl.ds(first + split, sr * res - split)]
+
+    def copy_of(owner, piece, target, index):
+        return pltpu.make_async_remote_copy(
+            src_ref=place(owner, piece),
+            dst_ref=place(owner, piece),
+            send_sem=send_sem.at[index],
+            recv_sem=recv_sem.at[owner, piece],
+            device_id=(group, target),
+            device_id_type=MESH,
+        )
+
+    def guarded(cond, action):
+        if cond is None:
+            action()
+        else:
+            pl.when(cond)(action)
+
+    def send(owner, piece, target, cond=None):
+        copy = copy_of(owner, piece, target, len(pending))
+        pending.append((copy, cond))
+        guarded(cond, copy.start)
+
+    def spread(owner, cond=None):
+        def action():
+            base = pl.multiple_of(owner * rows, 16)
+            for k in range(sr):
+                at = pl.ds(owner * sr + k, ch, stride=pad)
+                fa[at, :] = gf[pl.ds(base + k * ch, ch)].astype(f32)
+                fb[at, :] = gf[pl.ds(base + fr + k * ch, ch)].astype(f32)
+            masks = gf[pl.ds(base + 2 * fr, 16)].astype(f32)
+            for k in range(sr):
+                mf[pl.ds(owner * sr + k, 1), :] = masks[k:k + 1]
+        guarded(cond, action)
+
+    def arrive(owner, piece, cond=None):
+        guarded(cond, copy_of(owner, piece, sib, 0).wait_recv)
+
+    def both(a, b):
+        return a if b is None else jnp.logical_and(a, b)
+
+    def start(piece):
+        if piece == COT_X:
+            send(me, piece, xn)
+        send(me, piece, up, has_up)
+        send(me, piece, dn, has_dn)
+        if piece != COT_X:
+            send(me, piece, xn)
+        send(me, piece, sib)
+
+    def from_level(k, sign, same_column, piece):
+        zo = z + sign * k
+        cond = zo >= 0 if sign < 0 else zo <= levels - 1
+        owner = rank(zo, x if same_column else other, core)
+        arrive(owner, piece, cond)
+        if k < levels - 1 and (same_column or piece == COT_X):
+            onward, has_onward = (up, has_up) if sign < 0 else (dn, has_dn)
+            send(owner, piece, onward, both(has_onward, cond))
+        if same_column and piece != COT_X:
+            send(owner, piece, xn, cond)
+        send(owner, piece, sib, cond)
+        return owner, cond
+
+    def from_x(piece):
+        arrive(xn, piece)
+        if piece == COT_X:
+            send(xn, piece, up, has_up)
+            send(xn, piece, dn, has_dn)
+        send(xn, piece, sib)
+
+    start(FEATURES)
+
+    fa[...] = jnp.zeros_like(fa)
+    fb[...] = jnp.zeros_like(fb)
+    mf[...] = jnp.zeros_like(mf)
+    cb[...] = jnp.zeros_like(cb)
+    wf[...] = w_ref[...].astype(f32)
+    spread(me)
+
+    done = []
+    for k in range(1, levels):
+        for sign in (-1, 1):
+            done.append(from_level(k, sign, True, FEATURES))
+        if k == 1:
+            from_x(FEATURES)
+            done.append((xn, None))
+        for sign in (-1, 1):
+            done.append(from_level(k, sign, False, FEATURES))
+        if k == 1:
+            start(COT_X)
+            start(COT_Z)
+        for owner, cond in done:
+            spread(owner, cond)
+        done = []
+        if k == 1:
+            for p in range(hp):
+                for h in range(2):
+                    c = 2 * p + h
+                    wl[p * ch:(p + 1) * ch, h * lane:(h + 1) * lane] = (
+                        wf[pl.ds(c, ch, stride=ch), :].astype(bf16)
+                    )
+                    wr[p * ch:(p + 1) * ch, h * lane:(h + 1) * lane] = w_ref[c * ch:(c + 1) * ch]
+    for zz in range(levels):
+        for xx in range(2):
+            owner = rank(zz, xx, 1 - core)
+            arrive(owner, FEATURES)
+            spread(owner)
+
+    masks = mf[...].astype(bf16)
+    rn[...] = 1.0 / jnp.maximum(dot(masks, jnp.concatenate([masks, masks], 0), NT), 1.0)
+    bp[...] = fb[...].astype(bf16)
+
+    def fill_cot(k, block):
+        cb[k * lane:k * lane + res, 0:lane] = block
+        cb[k * lane + pad:k * lane + pad + res, lane:2 * lane] = block
+
+    def prob_step(v, carry):
+        base = pl.multiple_of(v * (2 * rows), 16)
+        features = jnp.concatenate([gf[pl.ds(base, fr)], gf[pl.ds(base + rows, fr)]], 0)
+        for p in range(0, hp, 2):
+            o = dot(features, bp[p * lane:(p + 2) * lane], NT)
+            for k in range(2 * sr):
+                scale = rn[pl.ds(v * (2 * sr) + k, 1), :]
+                for u in range(2):
+                    t[v, (p + u) * ch:(p + u + 1) * ch, k * lane:(k + 1) * lane] = (
+                        o[k * ch:(k + 1) * ch, u * lane:(u + 1) * lane] * scale
+                    ).astype(bf16)
+        return carry
+
+    def prob_steps(part):
+        lax.fori_loop(part * (n // 8), (part + 1) * (n // 8), prob_step, 0)
+
+    from_x(COT_X)
+    for k in range(1, levels):
+        for sign in (-1, 1):
+            from_level(k, sign, True, COT_Z)
+            from_level(k, sign, True, COT_X)
+        prob_steps(k - 1)
+        for sign in (-1, 1):
+            from_level(k, sign, False, COT_X)
+        if k == 1:
+            from_x(COT_Z)
+        for sign in (-1, 1):
+            from_level(k, sign, False, COT_Z)
+    prob_steps(3)
+    ap[...] = fa[...].astype(bf16)
+
+    width = sr * lane
+    scales = jnp.concatenate([rn[pl.ds(me * sr + k, 1), :] for k in range(sr)], 1)
+
+    def side(weights, features, out_ref):
+        og = (dot(weights, cb[:width], NT) * scales).astype(bf16)
+        flat = jnp.concatenate(
+            [
+                jnp.concatenate(
+                    [og[p * ch:(p + 1) * ch, k * lane:(k + 1) * lane] for p in range(hp)], 1
+                )
+                for k in range(sr)
+            ],
+            0,
+        )
+        grad = dot(flat, features[...])
+        grads = [grad[k * ch:(k + 1) * ch] * mf[pl.ds(me * sr + k, 1), :] for k in range(sr)]
+        fill = [jnp.zeros((ch, lane - fr), f32)] if fr < lane else []
+        turned = jnp.concatenate(
+            [
+                jnp.concatenate([grads[k][:, u * ch:(u + 1) * ch] for k in range(sr)] + fill, 1)
+                for u in range(q)
+            ],
+            0,
+        )
+        xf[...] = turned.T
+        for h in range(ch):
+            out_ref[:, h * lane:(h + 1) * lane] = xf[pl.ds(h, sr, stride=ch), :]
+
+    for k in range(sr):
+        fill_cot(k, cot_ref[k * res:(k + 1) * res])
+    side(wl[...], bp, lg_ref)
+    features = gf[pl.ds(slot, fr)]
+    for p in range(0, hp, 2):
+        o = dot(features, bp[p * lane:(p + 2) * lane], NT)
+        for k in range(sr):
+            for u in range(2):
+                acc[(p + u) * ch:(p + u + 1) * ch, k * lane:(k + 1) * lane] = (
+                    o[k * ch:(k + 1) * ch, u * lane:(u + 1) * lane] * scales[:, k * lane:(k + 1) * lane]
+                )
+    pairs = dot(acc[...].astype(bf16), wl[...], TN)
+    for k in range(sr):
+        pair_ref[k * res:(k + 1) * res] = (
+            pairs[k * lane:k * lane + res, :lane]
+            + pairs[k * lane + pad:k * lane + pad + res, lane:]
+            + bias_ref[...]
+        ).astype(bf16)
+
+    for zz in range(levels):
+        for xx in range(2):
+            arrive(rank(zz, xx, 1 - core), COT_X)
+            arrive(rank(zz, xx, 1 - core), COT_Z)
+
+    fc[...] = gc[...].astype(f32)
+    gb_ref[...] = jnp.sum(fc[...], axis=0, keepdims=True) * (1.0 / res)
+    for k in range(sr):
+        fill_cot(k, fc[pl.ds(me * sr + k, res, stride=res), :].astype(bf16))
+    side(wr[...], ap, rg_ref)
+
+    acc[:, :2 * lane] = jnp.zeros((ch * hp, 2 * lane), f32)
+
+    def weight_step(v, carry):
+        first = pl.multiple_of(v * (2 * sr * res), 16)
+        for k in range(2 * sr):
+            fill_cot(k, gc[pl.ds(first + k * res, res)])
+        acc[:, :2 * lane] += dot(t[v], cb[...])
+        return carry
+
+    lax.fori_loop(0, n // 2, weight_step, 0)
+    for p in range(hp):
+        for h in range(2):
+            gw_ref[pl.ds(2 * p + h, ch, stride=ch), :] = (
+                acc[p * ch:(p + 1) * ch, h * lane:(h + 1) * lane] * (1.0 / res)
+            )
+    for copy, cond in pending:
+        guarded(cond, copy.wait_send)
+
+
+def gathered_local(
+    left_features,
+    right_features,
+    alignment_mask,
+    projection_weight,
+    projection_bias,
+    pair_output_cotangent,
+):
+    f32, bf16 = jnp.float32, jnp.bfloat16
+    sr, width = left_features.shape
+    depth = alignment_mask.shape[1]
+    ch = width // depth
+    n = lax.axis_size("row")
+    res, hidden, lane = n * sr, ch * ch, 128
+    vmem = pl.BlockSpec(memory_space=pltpu.VMEM)
+    pair, lg, rg, gw, gb = pl.pallas_call(
+        functools.partial(fused_kernel, n // 4, n, sr, ch),
+        out_shape=(
+            jax.ShapeDtypeStruct((sr * res, lane), bf16),
+            jax.ShapeDtypeStruct((sr, width), f32),
+            jax.ShapeDtypeStruct((sr, width), f32),
+            jax.ShapeDtypeStruct((hidden, lane), f32),
+            jax.ShapeDtypeStruct((1, lane), f32),
+        ),
+        in_specs=[vmem] * 6,
+        out_specs=(vmem,) * 5,
+        scratch_shapes=[
+            pltpu.VMEM((n * (2 * sr * ch + 16), lane), bf16),
+            pltpu.VMEM((res * res, lane), bf16),
+            pltpu.VMEM((ch * 64, lane), f32),
+            pltpu.VMEM((ch * 64, lane), f32),
+            pltpu.VMEM((res * res, lane), f32),
+            pltpu.VMEM((64, lane), f32),
+            pltpu.VMEM((64, lane), f32),
+            pltpu.VMEM((ch * 64, lane), bf16),
+            pltpu.VMEM((ch * 64, lane), bf16),
+            pltpu.VMEM((hidden, lane), f32),
+            pltpu.VMEM((hidden // 2, 2 * lane), bf16),
+            pltpu.VMEM((hidden // 2, 2 * lane), bf16),
+            pltpu.VMEM((2 * sr * lane, 2 * lane), bf16),
+            pltpu.VMEM((n // 2, hidden // 2, 2 * sr * lane), bf16),
+            pltpu.VMEM((hidden // 2, max(sr, 2) * lane), f32),
+            pltpu.VMEM((lane, lane), f32),
+            pltpu.VMEM((16, lane), f32),
+            pltpu.SemaphoreType.DMA((96,)),
+            pltpu.SemaphoreType.DMA((n, 3)),
+        ],
+        compiler_params=pltpu.CompilerParams(
+            collective_id=0, has_side_effects=True, vmem_limit_bytes=48 * 1024 * 1024
+        ),
+        name="fused",
+    )(
+        left_features,
+        right_features,
+        alignment_mask,
+        projection_weight,
+        projection_bias.reshape(1, -1),
+        pair_output_cotangent.reshape(sr * res, -1),
+    )
+    return pair.reshape(sr, res, -1), lg, rg, gw, gb.reshape(-1)
+
+
+def streamed_local(
     left_features,
     right_features,
     alignment_mask,
@@ -136,4 +499,16 @@
         P("groups", None),
         P("groups"),
     )
+    size = mesh.shape["row"]
+
+    def local(left, right, mask, weight, bias, cot):
+        sr, depth = mask.shape
+        ch = left.shape[1] // depth
+        res = sr * size
+        fits = (
+            size == 16 and res % 16 == 0 and res <= 64 and ch == 32 and (sr * ch) % 16 == 0 and 2 <= sr <= 4
+            and depth == 128 and cot.shape[2] == 128
+        )
+        return (gathered_local if fits else streamed_local)(left, right, mask, weight, bias, cot)
+
     return jax.shard_map(local, mesh=mesh, in_specs=in_specs, out_specs=out_specs, check_vma=False)

time: 183 us -> 43.9 us (0.24)
  blocking collectives: 73.3 us -> 0 us
  waiting for transfers between devices: 57.7 us -> 0 us
  Pallas kernels: 0 us -> 35.8 us
  between operations: 14.9 us -> 0.66 us
  matrix products: 11.4 us -> 0 us
  local copies, waits for them, and re-layouts: 16.9 us -> 7.08 us
  other arithmetic: 7.93 us -> 0 us
    unnamed x2 -> x0, waiting for transfers between devices: 57.7 us -> none
    all_gather x2 -> x0, blocking collectives: 42 us -> none  [the longest x1 24.6 us: local(): lax.all_gather(right_masked, 'row', axis=0, tiled=True)]
    pallas_call x0 -> x1, Pallas kernels: none -> 35.8 us  [gathered_local(): pl.pallas_call(functools.partial(fused_kernel, n // 4, n, sr, ch), out_sh...]
    psum x1 -> x0, blocking collectives: 31.3 us -> none  [local(): weight_sum, bias_sum = lax.psum((weight_acc, bias_acc), 'row')]
    dot_general x19 -> x0, matrix products: 11.4 us -> none  [the longest x3 3.53 us: block_step(): jnp.dot(flat_prob, projection_weight, preferred_element_type=jnp.float32)]
    reshape x13 -> x0, local copies, waits for them, and re-layouts: 9.06 us -> none  [the longest x2 2.34 us: local(): grads_out.transpose(1, 0, 2, 3)]
    unnamed x13 -> x17, local copies, waits for them, and re-layouts: 1.38 us -> 7.08 us
    transpose x6 -> x0, local copies, waits for them, and re-layouts: 3.42 us -> none  [the longest x1 1.98 us: local(): jnp.einsum('ijce,isc->jse', outer_all, left_masked, preferred_element_typ...]
  transfers between devices with their start and end apart: 1 -> 0, of which waited for: 1 -> 0; matrix products, arithmetic and copies ran while one was open for 2% -> 0% of each run, Pallas kernels for 0% -> 0%
where the time goes in v2:
time: 43.9 us; the launch traced here: 43.6 us
  Pallas kernels  35.8 us (82%)
  local copies, waits for them, and re-layouts  7.08 us (16%)
  between operations  0.66 us (2%)
    pallas_call x1, Pallas kernels, gathered_local(): pl.pallas_call(functools.partial(fused_kernel, n // 4, n, sr, ch), out_sh...  35.8 us
    unnamed x17, local copies, waits for them, and re-layouts  7.08 us

profile of v2, /device:TPU:0, one launch (start us, length us, event | category | flops | bytes accessed | tf_op | source)
XLA Modules:
  0.0 43.6 jit_solution(5778676864359216586)
XLA Ops:
  0.6 0.0 copy-start.4
  0.6 0.0 copy-start.5
  0.7 0.7 %copy-done.4 = s32[3,128]{1,0:T(4,128)S(1)} copy-done((s32[3,128]{1,0:T(4,128)S(1)}, s32[3,128]{1,0:T(4,128)}, u32[]{:S(2)}) %copy-start.4) | copy-done | bytes 1560
  1.3 0.0 copy-done.5
  1.3 0.0 copy-start
  1.3 0.9 %copy-done = bf16[1024,128]{1,0:T(8,128)(2,1)S(1)} copy-done((bf16[1024,128]{1,0:T(8,128)(2,1)S(1)}, bf16[1024,128]{1,0:T(8,128)(2,1)}, u32[]{:S(2)}) %copy-start) | copy-done | bytes 262168
  2.3 0.0 copy-start.1
  2.3 0.8 %copy-done.1 = bf16[3,48,128]{2,1,0:T(8,128)(2,1)S(1)} copy-done((bf16[3,48,128]{2,1,0:T(8,128)(2,1)S(1)}, bf16[3,48,128]{2,1,0:T(8,128)(2,1)}, u32[]{:S(2)}) %copy-start.1) | copy-done | bytes 36888
  3.0 0.0 copy-start.2
  3.0 0.8 %copy-done.2 = bf16[3,4096]{1,0:T(4,128)(2,1)S(1)} copy-done((bf16[3,4096]{1,0:T(4,128)(2,1)S(1)}, bf16[3,4096]{1,0:T(4,128)(2,1)}, u32[]{:S(2)}) %copy-start.2) | copy-done | bytes 24600
  3.8 0.0 copy-start.3
  3.8 0.8 %copy-done.3 = bf16[3,4096]{1,0:T(4,128)(2,1)S(1)} copy-done((bf16[3,4096]{1,0:T(4,128)(2,1)S(1)}, bf16[3,4096]{1,0:T(4,128)(2,1)}, u32[]{:S(2)}) %copy-start.3) | copy-done | bytes 24600
  4.6 35.8 %fused.1 = (bf16[144,128]{1,0:T(8,128)(2,1)S(1)}, f32[3,4096]{1,0:T(4,128)S(1)}, f32[3,4096]{1,0:T(4,128)S(1)}, f32[1024,128]{1,0:T(8,128)S(1)}, f32[1,128]{1,0:T(1,128)S(1)}) custom-call(bf16[3,4096]{1,0:T(4,128)(2,1)S(1)} %copy-done.2, bf16[3,4096]{1,0:T(4,128)(2,1)S(1)} %copy-done.3, s32[3,128]{1,0:T(4,128)S(1)} %copy-done.4, ...), custom_call_target="tpu_custom_call" | custom-call | tf_op jit(solution)/shard_map/fused/pallas_call | solution.py:325
  40.4 0.6 %copy.16 = bf16[3,48,128]{2,1,0:T(8,128)(2,1)} copy(bf16[3,48,128]{2,1,0:T(8,128)(2,1)S(1)} %bitcast.4) | data formatting | bytes 73728
  41.0 0.6 %copy.17 = f32[3,4096]{1,0:T(4,128)} copy(f32[3,4096]{1,0:T(4,128)S(1)} %get-tuple-element.21) | data formatting | bytes 98304
  41.6 0.6 %copy.18 = f32[3,4096]{1,0:T(4,128)} copy(f32[3,4096]{1,0:T(4,128)S(1)} %get-tuple-element.22) | data formatting | bytes 98304
  42.3 0.8 %copy.19 = f32[1024,128]{1,0:T(8,128)} copy(f32[1024,128]{1,0:T(8,128)S(1)} %get-tuple-element.23) | data formatting | bytes 1048576
  43.1 0.5 %copy.20 = f32[128]{0:T(128)} copy(f32[128]{0:T(128)S(1)} %bitcast.7) | data formatting | bytes 1024
Async XLA Ops:
  0.6 0.7 %copy-start.4 = (s32[3,128]{1,0:T(4,128)S(1)}, s32[3,128]{1,0:T(4,128)}, u32[]{:S(2)}) copy-start(s32[3,128]{1,0:T(4,128)} %mask_ref.1) | copy-start | bytes 4612
  0.6 0.7 %copy-start.5 = (f32[128]{0:T(128)S(1)}, f32[128]{0:T(128)}, u32[]{:S(2)}) copy-start(f32[128]{0:T(128)} %param.10) | copy-start | bytes 1540
  1.3 1.0 %copy-start = (bf16[1024,128]{1,0:T(8,128)(2,1)S(1)}, bf16[1024,128]{1,0:T(8,128)(2,1)}, u32[]{:S(2)}) copy-start(bf16[1024,128]{1,0:T(8,128)(2,1)} %w_ref.1) | copy-start | bytes 786436
  2.3 0.8 %copy-start.1 = (bf16[3,48,128]{2,1,0:T(8,128)(2,1)S(1)}, bf16[3,48,128]{2,1,0:T(8,128)(2,1)}, u32[]{:S(2)}) copy-start(bf16[3,48,128]{2,1,0:T(8,128)(2,1)} %param.11) | copy-start | bytes 110596
  3.0 0.8 %copy-start.2 = (bf16[3,4096]{1,0:T(4,128)(2,1)S(1)}, bf16[3,4096]{1,0:T(4,128)(2,1)}, u32[]{:S(2)}) copy-start(bf16[3,4096]{1,0:T(4,128)(2,1)} %left_ref.1) | copy-start | bytes 73732
  3.8 0.8 %copy-start.3 = (bf16[3,4096]{1,0:T(4,128)(2,1)S(1)}, bf16[3,4096]{1,0:T(4,128)(2,1)}, u32[]{:S(2)}) copy-start(bf16[3,4096]{1,0:T(4,128)(2,1)} %right_ref.1) | copy-start | bytes 73732

commit v3 on v1

--- a/solution.py
+++ b/solution.py
@@ -13,11 +13,23 @@
 TN = (((0,), (0,)), ((), ()))
 
 
-def gather_kernel(levels, pack_ref, out_ref, send_sem, recv_sem, own_sem):
+def gather_kernel(
+    levels, sr, ch, left_hbm, right_hbm, mask_hbm, cot_hbm, out_ref,
+    left_ref, right_ref, mask_ref, xf, m16, send_sem, recv_sem, own_sem,
+):
+    f32, bf16 = jnp.float32, jnp.bfloat16
+    lane, q = 128, 128 // ch
+    fr = sr * ch
+    cot_rows = cot_hbm.shape[0]
+    rows = out_ref.shape[0] // (levels * 4)
+    loads = [
+        pltpu.make_async_copy(source, target, own_sem.at[k])
+        for k, (source, target) in enumerate(
+            ((left_hbm, left_ref), (right_hbm, right_ref), (mask_hbm, mask_ref))
+        )
+    ]
     group = lax.axis_index("groups")
     me = lax.axis_index("row")
-    rows = pack_ref.shape[0]
-    half_rows = rows // 2
     core = lax.rem(me, 2)
     x = lax.rem(me // 2, 2)
     z = me // 4
@@ -38,17 +50,51 @@
     greet(xn)
     pl.when(has_up)(lambda: greet(up))
     pl.when(has_dn)(lambda: greet(dn))
-    own = pltpu.make_async_copy(pack_ref, out_ref.at[pl.ds(me * rows, rows)], own_sem)
-    own.start()
+    slot = pl.multiple_of(me * rows, 16)
+    cot_copy = pltpu.make_async_copy(
+        cot_hbm, out_ref.at[pl.ds(slot + 2 * fr, cot_rows)], own_sem.at[3]
+    )
+    for load in loads:
+        load.start()
+    cot_copy.start()
+
+    m16[...] = jnp.zeros_like(m16)
+    xf[...] = jnp.zeros_like(xf)
+    for load in loads:
+        load.wait()
+    m16[:sr] = mask_ref[...].astype(f32)
+    row_at = lax.broadcasted_iota(jnp.int32, (lane, lane), 0)
+    lane_at = lax.broadcasted_iota(jnp.int32, (lane, lane), 1)
+    order = ((row_at % q) * (lane // q) + row_at // q == lane_at).astype(bf16)
+    own_mask = jnp.dot(m16[...].astype(bf16), order, preferred_element_type=f32)
+    out_ref[pl.ds(slot + 2 * fr + cot_rows, 16)] = own_mask.astype(bf16)
+    for side_index, ref in enumerate((left_ref, right_ref)):
+        for h in range(ch):
+            xf[pl.ds(h, sr, stride=ch), :] = ref[:, h * lane:(h + 1) * lane].astype(f32)
+        turned = xf[...].T
+        for i in range(sr):
+            block = jnp.concatenate(
+                [turned[u * ch:(u + 1) * ch, i * ch:(i + 1) * ch] for u in range(q)], 1
+            )
+            out_ref[pl.ds(slot + side_index * fr + i * ch, ch)] = (block * own_mask[i:i + 1]).astype(bf16)
+    tail = slot + 2 * fr + cot_rows + 16
+    spare = rows - 2 * fr - cot_rows - 16
+    if spare:
+        out_ref[pl.ds(tail, spare)] = jnp.zeros((spare, lane), bf16)
+    cot_copy.wait()
+
     pl.semaphore_wait(barrier, 2 + has_up.astype(jnp.int32) + has_dn.astype(jnp.int32))
 
     pending = []
+    cut = rows // 6 // 16 * 16
+    mid = (rows - cut) // 2 // 16 * 16
 
     def place(owner, half):
-        return out_ref.at[pl.ds(owner * rows + half * half_rows, half_rows)]
-
-    def copy_of(owner, half, target, index, local):
-        src = pack_ref.at[pl.ds(half * half_rows, half_rows)] if local else place(owner, half)
+        first, count = ((0, cut), (cut, mid), (cut + mid, rows - cut - mid))[half]
+        return out_ref.at[pl.ds(pl.multiple_of(owner * rows + first, 16), count)]
+
+    def copy_of(owner, half, target, index):
+        src = place(owner, half)
         return pltpu.make_async_remote_copy(
             src_ref=src,
             dst_ref=place(owner, half),
@@ -58,8 +104,8 @@
             device_id_type=MESH,
         )
 
-    def send(owner, half, target, cond=None, local=False):
-        copy = copy_of(owner, half, target, len(pending), local)
+    def send(owner, half, target, cond=None):
+        copy = copy_of(owner, half, target, len(pending))
         pending.append((copy, cond))
         if cond is None:
             copy.start()
@@ -67,7 +113,7 @@
             pl.when(cond)(copy.start)
 
     def arrive(owner, half, cond=None):
-        copy = copy_of(owner, half, sib, 0, False)
+        copy = copy_of(owner, half, sib, 0)
         if cond is None:
             copy.wait_recv()
         else:
@@ -76,14 +122,15 @@
     def both(a, b):
         return a if b is None else jnp.logical_and(a, b)
 
-    send(me, 0, xn, local=True)
-    send(me, 1, up, has_up, local=True)
-    send(me, 1, dn, has_dn, local=True)
-    send(me, 0, up, has_up, local=True)
-    send(me, 0, dn, has_dn, local=True)
-    send(me, 1, xn, local=True)
-    send(me, 0, sib, local=True)
-    send(me, 1, sib, local=True)
+    send(me, 0, xn)
+    for piece in (1, 2):
+        send(me, piece, up, has_up)
+        send(me, piece, dn, has_dn)
+        send(me, piece, xn)
+    send(me, 0, up, has_up)
+    send(me, 0, dn, has_dn)
+    for piece in (1, 2, 0):
+        send(me, piece, sib)
 
     arrive(xn, 0)
     send(xn, 0, up, has_up)
@@ -99,65 +146,69 @@
             onward, has_onward = (up, has_up) if sign < 0 else (dn, has_dn)
             if k < levels - 1:
                 send(owner, half, onward, both(has_onward, cond))
-        if half == 1 and xx is x:
+        if half != 0 and xx is x:
             send(owner, half, xn, cond)
         send(owner, half, sib, cond)
 
     other = 1 - x
     for k in range(1, levels):
-        for sign in (-1, 1):
-            from_level(k, sign, x, 1)
-        for sign in (-1, 1):
-            from_level(k, sign, x, 0)
+        for piece in (1, 2, 0):
+            for sign in (-1, 1):
+                from_level(k, sign, x, piece)
         if k == 1:
-            arrive(xn, 1)
-            send(xn, 1, sib)
-        for sign in (-1, 1):
-            from_level(k, sign, other, 0)
-        for sign in (-1, 1):
-            from_level(k, sign, other, 1)
+            for piece in (1, 2):
+                arrive(xn, piece)
+                send(xn, piece, sib)
+        for piece in (0, 1, 2):
+            for sign in (-1, 1):
+                from_level(k, sign, other, piece)
 
     for zz in range(levels):
         for xx in range(2):
-            for half in range(2):
-                arrive(rank(zz, xx, 1 - core), half)
+            for piece in range(3):
+                arrive(rank(zz, xx, 1 - core), piece)
     for copy, cond in pending:
         if cond is None:
             copy.wait_send()
         else:
             pl.when(cond)(copy.wait_send)
-    own.wait()
-
-
-def gather(pack, size):
-    levels = size // 4
-    rows, lanes = pack.shape
+
+
+def gather(left, right, mask, cot, size, sr, ch, rows):
+    lane = cot.shape[1]
+    any_space = pl.BlockSpec(memory_space=pl.ANY)
     return pl.pallas_call(
-        functools.partial(gather_kernel, levels),
-        out_shape=jax.ShapeDtypeStruct((size * rows, lanes), pack.dtype),
-        in_specs=[pl.BlockSpec(memory_space=pltpu.VMEM)],
+        functools.partial(gather_kernel, size // 4, sr, ch),
+        out_shape=jax.ShapeDtypeStruct((size * rows, lane), cot.dtype),
+        in_specs=[any_space] * 4,
         out_specs=pl.BlockSpec(memory_space=pltpu.VMEM),
         scratch_shapes=[
-            pltpu.SemaphoreType.DMA((64,)),
-            pltpu.SemaphoreType.DMA((size, 2)),
-            pltpu.SemaphoreType.DMA,
+            pltpu.VMEM(left.shape, left.dtype),
+            pltpu.VMEM(right.shape, right.dtype),
+            pltpu.VMEM(mask.shape, mask.dtype),
+            pltpu.VMEM((lane, lane), jnp.float32),
+            pltpu.VMEM((16, lane), jnp.float32),
+            pltpu.SemaphoreType.DMA((128,)),
+            pltpu.SemaphoreType.DMA((size, 3)),
+            pltpu.SemaphoreType.DMA((4,)),
         ],
         compiler_params=pltpu.CompilerParams(
             collective_id=0, has_side_effects=True, vmem_limit_bytes=32 * 1024 * 1024
         ),
         name="gather",
-    )(pack)
+    )(left, right, mask, cot)
 
 
 def compute_kernel(
     n, sr, ch, rows, g, w_ref, bias_ref, pair_ref, lg_ref, rg_ref, gw_ref, gb_ref,
-    fa, fb, fc, mf, rn, bp, ap, wf, wl, wr, cb, t, acc,
+    fa, fb, fc, mf, rn, bp, ap, wf, wl, wr, cb, t, acc, xf,
 ):
     f32, bf16 = jnp.float32, jnp.bfloat16
     me = lax.axis_index("row")
     res = n * sr
     pad = 64
     lane = 128
+    q = lane // ch
     hp = ch // 2
     fr = sr * ch
     cot_at, mask_at = 2 * fr, 2 * fr + sr * res
@@ -184,9 +235,9 @@
     wf[...] = w_ref[...].astype(f32)
     for p in range(hp):
         for h in range(2):
-            q = 2 * p + h
-            wl[p * ch:(p + 1) * ch, h * lane:(h + 1) * lane] = wf[pl.ds(q, ch, stride=ch), :].astype(bf16)
-            wr[p * ch:(p + 1) * ch, h * lane:(h + 1) * lane] = w_ref[q * ch:(q + 1) * ch]
+            c = 2 * p + h
+            wl[p * ch:(p + 1) * ch, h * lane:(h + 1) * lane] = wf[pl.ds(c, ch, stride=ch), :].astype(bf16)
+            wr[p * ch:(p + 1) * ch, h * lane:(h + 1) * lane] = w_ref[c * ch:(c + 1) * ch]
 
     gb_ref[...] = jnp.sum(fc[...], axis=0, keepdims=True) * (1.0 / res)
     cb[...] = jnp.zeros_like(cb)
@@ -226,7 +277,7 @@
     width = sr * lane
     scales = jnp.concatenate([rn[pl.ds(me * sr + k, 1), :] for k in range(sr)], 1)
 
-    def side(weights, features):
+    def side(weights, features, out_ref):
         og = (dot(weights, cb[:width], NT) * scales).astype(bf16)
         flat = jnp.concatenate(
             [
@@ -237,25 +288,34 @@
             ],
             0,
         )
-        return dot(flat, features[...])
+        grad = dot(flat, features[...])
+        grads = [grad[k * ch:(k + 1) * ch] * mf[pl.ds(me * sr + k, 1), :] for k in range(sr)]
+        fill = [jnp.zeros((ch, lane - fr), f32)] if fr < lane else []
+        turned = jnp.concatenate(
+            [
+                jnp.concatenate([grads[k][:, u * ch:(u + 1) * ch] for k in range(sr)] + fill, 1)
+                for u in range(q)
+            ],
+            0,
+        )
+        xf[...] = turned.T
+        for h in range(ch):
+            out_ref[:, h * lane:(h + 1) * lane] = xf[pl.ds(h, sr, stride=ch), :]
 
     fill_prob(g[pl.ds(base, fr)], me * sr, sr)
     for k in range(sr):
         fill_cot(k, g[pl.ds(base + cot_at + k * res, res)])
     pairs = dot(t[:, :width], wl[...], TN)
-    lg = side(wl[...], bp)
+    side(wl[...], bp, lg_ref)
     for k in range(sr):
         pair_ref[k * res:(k + 1) * res] = (
             pairs[k * lane:k * lane + res, :lane]
             + pairs[k * lane + pad:k * lane + pad + res, lane:]
             + bias_ref[...]
         ).astype(bf16)
-        lg_ref[k * ch:(k + 1) * ch] = lg[k * ch:(k + 1) * ch] * mf[pl.ds(me * sr + k, 1), :]
     for k in range(sr):
         fill_cot(k, fc[pl.ds(me * sr + k, res, stride=res), :].astype(bf16))
-    rg = side(wr[...], ap)
-    for k in range(sr):
-        rg_ref[k * ch:(k + 1) * ch] = rg[k * ch:(k + 1) * ch] * mf[pl.ds(me * sr + k, 1), :]
+    side(wr[...], ap, rg_ref)
 
 
 def compute(g, weight, bias, n, sr, ch, rows):
@@ -266,8 +326,8 @@
         functools.partial(compute_kernel, n, sr, ch, rows),
         out_shape=(
             jax.ShapeDtypeStruct((sr * res, lane), bf16),
-            jax.ShapeDtypeStruct((sr * ch, lane), f32),
-            jax.ShapeDtypeStruct((sr * ch, lane), f32),
+            jax.ShapeDtypeStruct((sr, ch * lane), f32),
+            jax.ShapeDtypeStruct((sr, ch * lane), f32),
             jax.ShapeDtypeStruct((hidden, lane), f32),
             jax.ShapeDtypeStruct((1, lane), f32),
         ),
@@ -287,6 +347,7 @@
             pltpu.VMEM((2 * sr * lane, 2 * lane), bf16),
             pltpu.VMEM((hidden // 2, 2 * sr * lane), bf16),
             pltpu.VMEM((hidden // 2, 2 * lane), f32),
+            pltpu.VMEM((lane, lane), f32),
         ],
         compiler_params=pltpu.CompilerParams(vmem_limit_bytes=40 * 1024 * 1024),
         name="compute",
@@ -306,30 +367,15 @@
     ch = width // depth
     n = lax.axis_size("row")
     res = n * sr
-    mask = alignment_mask.astype(jnp.bfloat16)
-
-    def by_channel(features):
-        masked = features.reshape(sr, depth, ch) * mask[:, :, None]
-        return masked.transpose(0, 2, 1).reshape(sr * ch, depth)
-
-    parts = [
-        by_channel(left_features),
-        by_channel(right_features),
-        pair_output_cotangent.reshape(sr * res, -1),
-        mask,
-    ]
-    used = sum(part.shape[0] for part in parts)
-    rows = -(-used // 32) * 32
-    parts.append(jnp.zeros((rows - used, depth), jnp.bfloat16))
-    pack = jnp.concatenate(parts, 0)
+    rows = -(-(2 * sr * ch + sr * res + 16) // 32) * 32
+    gathered = gather(
+        left_features, right_features, alignment_mask,
+        pair_output_cotangent.reshape(sr * res, -1), n, sr, ch, rows,
+    )
     pair, lg, rg, gw, gb = compute(
-        gather(pack, n), projection_weight, projection_bias.reshape(1, -1), n, sr, ch, rows
-    )
-
-    def by_row(grad):
-        return grad.reshape(sr, ch, depth).transpose(0, 2, 1).reshape(sr, width)
-
-    return pair.reshape(sr, res, -1), by_row(lg), by_row(rg), gw, gb.reshape(-1)
+        gathered, projection_weight, projection_bias.reshape(1, -1), n, sr, ch, rows
+    )
+    return pair.reshape(sr, res, -1), lg, rg, gw, gb.reshape(-1)
 
 
 def streamed_local(
@@ -470,7 +516,7 @@
         res = sr * size
         fits = (
             size == 16 and res % 16 == 0 and res <= 64 and ch == 32 and (sr * ch) % 16 == 0
-            and depth == 128 and cot.shape[2] == 128 and sr <= 16
+            and depth == 128 and cot.shape[2] == 128 and sr <= 4
         )
         return (gathered_local if fits else streamed_local)(left, right, mask, weight, bias, cot)
 

time: 34.7 us -> 33.3 us (0.960)
  local copies, waits for them, and re-layouts: 4.68 us -> 3.01 us
  Pallas kernels: 28.1 us -> 29.3 us
  other arithmetic: 0.85 us -> 0 us
    reshape x6 -> x0, local copies, waits for them, and re-layouts: 3.55 us -> none  [the longest x4 1.8 us: by_row(): return grad.reshape(sr, ch, depth).transpose(0, 2, 1).reshape(sr, width)]
    unnamed x4 -> x12, local copies, waits for them, and re-layouts: 0.01 us -> 3.01 us
    pallas_call x1, Pallas kernels: 19.1 us -> 20.1 us  [gather(): pl.pallas_call(functools.partial(gather_kernel, size // 4, sr, ch), out_s...]
    concatenate x1 -> x0, local copies, waits for them, and re-layouts: 0.94 us -> none  [gathered_local(): pack = jnp.concatenate(parts, 0)]
    convert_element_type x1 -> x0, other arithmetic: 0.73 us -> none  [gathered_local(): mask = alignment_mask.astype(jnp.bfloat16)]
where the time goes in v3:
time: 33.3 us; the launch traced here: 33 us
  Pallas kernels  29.3 us (88%)
  local copies, waits for them, and re-layouts  3.01 us (9%)
  between operations  0.68 us (2%)
    pallas_call x1, Pallas kernels, gather(): pl.pallas_call(functools.partial(gather_kernel, size // 4, sr, ch), out_s...  20.1 us
    pallas_call x1, Pallas kernels, compute(): pl.pallas_call(functools.partial(compute_kernel, n, sr, ch, rows), out_sh...  9.25 us
    unnamed x12, local copies, waits for them, and re-layouts  3.01 us

profile of v3, /device:TPU:0, one launch (start us, length us, event | category | flops | bytes accessed | tf_op | source)
XLA Modules:
  0.0 33.0 jit_solution(1829720114441466571)
XLA Ops:
  0.6 0.0 copy-start
  0.6 0.0 copy-start.1
  0.7 0.8 %copy-done.1 = bf16[3,48,128]{2,1,0:T(8,128)(2,1)S(1)} copy-done((bf16[3,48,128]{2,1,0:T(8,128)(2,1)S(1)}, bf16[3,48,128]{2,1,0:T(8,128)(2,1)}, u32[]{:S(2)}) %copy-start.1) | copy-done | bytes 36888
  1.5 0.0 copy-start.2
  1.5 0.8 %copy-done.2 = bf16[3,4096]{1,0:T(4,128)(2,1)S(1)} copy-done((bf16[3,4096]{1,0:T(4,128)(2,1)S(1)}, bf16[3,4096]{1,0:T(4,128)(2,1)}, u32[]{:S(2)}) %copy-start.2) | copy-done | bytes 24600
  2.2 0.0 copy-start.3
  2.2 0.8 %copy-done.3 = bf16[3,4096]{1,0:T(4,128)(2,1)S(1)} copy-done((bf16[3,4096]{1,0:T(4,128)(2,1)S(1)}, bf16[3,4096]{1,0:T(4,128)(2,1)}, u32[]{:S(2)}) %copy-start.3) | copy-done | bytes 24600
  3.0 0.0 copy-start.4
  3.0 0.7 %copy-done.4 = s32[3,128]{1,0:T(4,128)S(1)} copy-done((s32[3,128]{1,0:T(4,128)S(1)}, s32[3,128]{1,0:T(4,128)}, u32[]{:S(2)}) %copy-start.4) | copy-done | bytes 1560
  3.7 0.0 copy-start.5
  3.7 20.1 %gather.1.g = bf16[5632,128]{1,0:T(8,128)(2,1)S(1)} custom-call(bf16[3,4096]{1,0:T(4,128)(2,1)S(1)} %copy-done.2, bf16[3,4096]{1,0:T(4,128)(2,1)S(1)} %copy-done.3, s32[3,128]{1,0:T(4,128)S(1)} %copy-done.4, bf16[144,128]{1,0:T(8,128)(2,1)S(1)} %bitcast.4), custom_call_target="tpu_custom_call" | custom-call | tf_op jit(solution)/shard_map/gather/pallas_call | solution.py:180
  23.8 0.0 copy-done
  23.8 0.0 copy-done.5
  23.8 9.3 %compute.1 = (bf16[144,128]{1,0:T(8,128)(2,1)}, f32[3,4096]{1,0:T(4,128)}, f32[3,4096]{1,0:T(4,128)}, f32[1024,128]{1,0:T(8,128)}, f32[1,128]{1,0:T(1,128)}) custom-call(bf16[5632,128]{1,0:T(8,128)(2,1)S(1)} %gather.1.g, bf16[1024,128]{1,0:T(8,128)(2,1)S(1)} %copy-done, f32[1,128]{1,0:T(1,128)S(1)} %bitcast.5), custom_call_target="tpu_custom_call" | custom-call | tf_op jit(solution)/shard_map/compute/pallas_call | solution.py:325
Async XLA Ops:
  0.6 23.1 %copy-start = (bf16[1024,128]{1,0:T(8,128)(2,1)S(1)}, bf16[1024,128]{1,0:T(8,128)(2,1)}, u32[]{:S(2)}) copy-start(bf16[1024,128]{1,0:T(8,128)(2,1)} %w_ref.1) | copy-start | bytes 786436
  0.6 0.8 %copy-start.1 = (bf16[3,48,128]{2,1,0:T(8,128)(2,1)S(1)}, bf16[3,48,128]{2,1,0:T(8,128)(2,1)}, u32[]{:S(2)}) copy-start(bf16[3,48,128]{2,1,0:T(8,128)(2,1)} %param.11) | copy-start | bytes 110596
  1.5 0.8 %copy-start.2 = (bf16[3,4096]{1,0:T(4,128)(2,1)S(1)}, bf16[3,4096]{1,0:T(4,128)(2,1)}, u32[]{:S(2)}) copy-start(bf16[3,4096]{1,0:T(4,128)(2,1)} %left_hbm.1) | copy-start | bytes 73732
  2.2 0.8 %copy-start.3 = (bf16[3,4096]{1,0:T(4,128)(2,1)S(1)}, bf16[3,4096]{1,0:T(4,128)(2,1)}, u32[]{:S(2)}) copy-start(bf16[3,4096]{1,0:T(4,128)(2,1)} %right_hbm.1) | copy-start | bytes 73732
  3.0 0.7 %copy-start.4 = (s32[3,128]{1,0:T(4,128)S(1)}, s32[3,128]{1,0:T(4,128)}, u32[]{:S(2)}) copy-start(s32[3,128]{1,0:T(4,128)} %mask_hbm.1) | copy-start | bytes 4612
  3.7 20.1 %copy-start.5 = (f32[128]{0:T(128)S(1)}, f32[128]{0:T(128)}, u32[]{:S(2)}) copy-start(f32[128]{0:T(128)} %param.10) | copy-start | bytes 1540
